TPU v7x, 32 devices: a whole 2x2x4 slice. The times are simulated.
32 devices in a mesh: grp: 2 (over y), blk: 4 (over z), seq: 2 (over x), col: 2 (over core).
Axes of the slice: x: 2, y: 2, z: 4, core: 2. Of those that a mesh axis runs over, the one named last changes fastest.
Arguments:
- activations: bfloat16 [2048, 6912], P(('grp', 'blk', 'seq'), 'col'), parts along dimension 0, may hold values from -6 to 6
- output_grads: bfloat16 [2048, 5120], P(('grp', 'blk', 'seq')), parts along dimension 0, may hold values from -6 to 6
- queries: float32 [2, 6912, 5120], P('grp', ('col', 'blk'), 'seq'), parts along dimension 0, may hold values from -6.1035156e-05 to 6.1035156e-05
- lengths: int32 [8], P(('grp', 'blk')), parts along dimension 0, may hold values from 32 to 256, as said below
- assignment: int32 [8], P('grp'), parts along dimension 0, may hold values from 0 to 3, each once
Outputs:
- scores: float32 [1, 8], P(None, ('grp', 'blk')), parts along dimension 1
There are 2 independent parts, one for each index of `grp`. A program takes and returns all parts, laid end to end along the dimension named above; each array names one. Nothing has to cross between parts.
Inputs may be any that keep to these rules, and one draw needn't show every extreme that they name: `lengths`: one slot of each part holds a document of exactly 256 valid tokens. `assignment`: each document is held by exactly one slot.
All inputs are finite; a program needn't handle non-finite values.
Results may differ from a plain program's by a relative error of at most 0.0003.
Values may be sent and summed in bfloat16 or wider, within the bound.
A program may use at most 128 MiB of HBM per device.

v0:
```python
import jax
import jax.numpy as jnp
from jax import lax
from jax.sharding import PartitionSpec as P


def shifted(value, axis, steps):
    count = lax.axis_size(axis)
    pairs = [(source, (source + steps) % count) for source in range(count)]
    return lax.ppermute(value, axis, pairs)


def on_device(activations, output_grads, queries, lengths, assignment):
    blocks = lax.axis_size("blk")
    own_blk = lax.axis_index("blk")
    own_seq = lax.axis_index("seq")
    seq_rows = output_grads.shape[0]
    panel_width = queries.shape[1]
    positions = own_seq * seq_rows + jnp.arange(seq_rows, dtype=jnp.int32)
    masked = jnp.where(
        (positions < lengths[0])[:, None], output_grads, jnp.zeros_like(output_grads)
    )
    deltas = lax.all_to_all(masked, "seq", split_axis=1, concat_axis=0, tiled=True)

    def panel_score(query_piece, panel_index):
        offset = panel_index * panel_width
        columns = lax.dynamic_slice_in_dim(activations, offset, panel_width, 1)
        grad_block = lax.dot_general(
            lax.all_gather(columns, "seq", axis=0, tiled=True),
            deltas,
            (((0,), (0,)), ((), ())),
            preferred_element_type=jnp.float32,
        )
        return jnp.einsum("qfd,fd->q", query_piece, grad_block, precision=lax.Precision.HIGHEST)

    def add_score(running, partial_value):
        return running + lax.psum(partial_value, ("seq", "col"))

    def send_forward(query_piece):
        return shifted(query_piece, "blk", 1)

    running = add_score(jnp.zeros((queries.shape[0],), jnp.float32), panel_score(queries, own_blk))

    def one_step(step_index, loop_state):
        query_piece, running = loop_state
        query_piece = send_forward(query_piece)
        panel_index = (own_blk - step_index) % blocks
        return (query_piece, add_score(running, panel_score(query_piece, panel_index)))

    query_piece, running = lax.fori_loop(1, blocks, one_step, (queries, running))
    slot_values = lax.all_gather(running[:, None], "blk", axis=1, tiled=True)
    chosen = assignment[None, :] == own_blk
    return jnp.sum(jnp.where(chosen, slot_values, 0.0), axis=1, keepdims=True)


def solution(mesh):
    in_specs = (
        P(("grp", "blk", "seq"), "col"),
        P(("grp", "blk", "seq"), None),
        P("grp", ("col", "blk"), "seq"),
        P(("grp", "blk")),
        P("grp"),
    )
    out_specs = P(None, ("grp", "blk"))
    return jax.shard_map(
        on_device, mesh=mesh, in_specs=in_specs, out_specs=out_specs, check_vma=False
    )
```

profile of v0, /device:TPU:0, one launch (start us, length us, event | category | flops | bytes accessed | tf_op | source)
XLA Modules:
  0.0 709.3 jit_solution(2219935336389311228)
XLA Ops:
  0.0 7.7 %copy.34 = f32[1,864,2560]{2,1,0:T(8,128)} copy(f32[1,864,2560]{2,1,0:T(8,128)} %param.9) | data formatting | bytes 17694720
  8.3 0.2 broadcast_select_fusion
  8.5 1.2 copy.21
  9.7 4.2 all-to-all-start
  13.9 0.7 dynamic-slice
  14.6 0.1 constant_dynamic-slice_fusion.1
  14.7 21.4 %all_gather.16 = bf16[256,864]{1,0:T(8,128)(2,1)S(1)} all-gather(bf16[128,864]{1,0:T(8,128)(2,1)S(1)} %constant_dynamic-slice_fusion.1), channel_id=1, replica_groups=mesh['grp'=2,'blk'=4,'seq'=2,'col'=2] {'seq'}, dimensions={0}, use_global_device_ids=true | all-gather | bytes 663552 | tf_op jit(solution)/shard_map/all_gather | solution.py:29
  36.1 6.7 fusion.1
  42.8 6.4 psum.21
  49.2 649.8 %while.17 = (s32[]{:T(128)}, f32[1,864,2560]{2,1,0:T(8,128)}, f32[1]{0:T(128)}, s32[]{:T(128)}, bf16[128,3456]{1,0:T(8,128)(2,1)S(1)}, /*index=5*/bf16[256,2560]...) while((s32[]{:T(128)}, f32[1,864,2560]{2,1,0:T(8,128)}, ...), condition=%wide.region_3.4_spmd, body=%wide.region_1.3_spmd.sunk | while | flops 1136885760 | bytes 64790872 | solution.py:50
  49.2 1.8 collective-permute-start
  51.0 0.1 constant_dynamic-slice_fusion.3
  51.1 7.7 %all_gather.19 = bf16[256,864]{1,0:T(8,128)(2,1)S(1)} all-gather(bf16[128,864]{1,0:T(8,128)(2,1)S(1)} %constant_dynamic-slice_fusion.3), channel_id=1, replica_groups=mesh['grp'=2,'blk'=4,'seq'=2,'col'=2] {'seq'}, dimensions={0}, use_global_device_ids=true | all-gather | bytes 663552 | tf_op jit(solution)/shard_map/while/body/eval_jaxpr/all_gather | solution.py:29
  58.8 184.7 %collective-permute-done = f32[1,864,2560]{2,1,0:T(8,128)} collective-permute-done((f32[1,864,2560]{2,1,0:T(8,128)}, f32[1,864,2560]{2,1,0:T(8,128)}, u32[]{:S(2)}, u32[]{:S(2)}) %collective-permute-start) | collective-permute-done | bytes 8847392 | tf_op jit(solution)/shard_map/while/body/eval_jaxpr/ppermute | solution.py:10
  243.6 6.6 fusion.12
  250.2 6.4 psum.23
  257.9 7.5 %copy.29 = f32[1,864,2560]{2,1,0:T(8,128)} copy(f32[1,864,2560]{2,1,0:T(8,128)} %collective-permute-done) | data formatting | bytes 17694720 | tf_op jit(solution)/shard_map/while
  266.0 0.1 constant_dynamic-slice_fusion.3
  266.1 7.9 %all_gather.19 = bf16[256,864]{1,0:T(8,128)(2,1)S(1)} all-gather(bf16[128,864]{1,0:T(8,128)(2,1)S(1)} %constant_dynamic-slice_fusion.3), channel_id=1, replica_groups=mesh['grp'=2,'blk'=4,'seq'=2,'col'=2] {'seq'}, dimensions={0}, use_global_device_ids=true | all-gather | bytes 663552 | tf_op jit(solution)/shard_map/while/body/eval_jaxpr/all_gather | solution.py:29
  274.1 186.0 %collective-permute-done = f32[1,864,2560]{2,1,0:T(8,128)} collective-permute-done((f32[1,864,2560]{2,1,0:T(8,128)}, f32[1,864,2560]{2,1,0:T(8,128)}, u32[]{:S(2)}, u32[]{:S(2)}) %collective-permute-start) | collective-permute-done | bytes 8847392 | tf_op jit(solution)/shard_map/while/body/eval_jaxpr/ppermute | solution.py:10
  460.0 6.6 fusion.12
  466.6 6.5 psum.23
  474.4 7.5 %copy.29 = f32[1,864,2560]{2,1,0:T(8,128)} copy(f32[1,864,2560]{2,1,0:T(8,128)} %collective-permute-done) | data formatting | bytes 17694720 | tf_op jit(solution)/shard_map/while
  482.5 0.1 constant_dynamic-slice_fusion.3
  482.6 7.9 %all_gather.19 = bf16[256,864]{1,0:T(8,128)(2,1)S(1)} all-gather(bf16[128,864]{1,0:T(8,128)(2,1)S(1)} %constant_dynamic-slice_fusion.3), channel_id=1, replica_groups=mesh['grp'=2,'blk'=4,'seq'=2,'col'=2] {'seq'}, dimensions={0}, use_global_device_ids=true | all-gather | bytes 663552 | tf_op jit(solution)/shard_map/while/body/eval_jaxpr/all_gather | solution.py:29
  490.5 186.0 %collective-permute-done = f32[1,864,2560]{2,1,0:T(8,128)} collective-permute-done((f32[1,864,2560]{2,1,0:T(8,128)}, f32[1,864,2560]{2,1,0:T(8,128)}, u32[]{:S(2)}, u32[]{:S(2)}) %collective-permute-start) | collective-permute-done | bytes 8847392 | tf_op jit(solution)/shard_map/while/body/eval_jaxpr/ppermute | solution.py:10
  676.5 6.6 fusion.12
  683.1 6.5 psum.23
  690.9 7.5 %copy.29 = f32[1,864,2560]{2,1,0:T(8,128)} copy(f32[1,864,2560]{2,1,0:T(8,128)} %collective-permute-done) | data formatting | bytes 17694720 | tf_op jit(solution)/shard_map/while
  699.0 1.4 dynamic-update-slice
  700.4 8.3 %all-reduce = f32[4]{0:T(128)S(1)} all-reduce(f32[4]{0:T(128)S(1)} %dynamic-update-slice), channel_id=2, replica_groups=mesh['grp'=2,'blk'=4,'seq'=2,'col'=2] {'blk'}, use_global_device_ids=true, to_apply=%add | all-reduce | flops 4 | bytes 32
  708.7 0.6 fusion.2
  (13 shorter events, 0.0 us)
Async XLA Ops:
  0.0 13.9 %copy-start.3 = (u32[32]{0:T(128)S(1)}, u32[32]{0:T(128)}, u32[]{:S(2)}) copy-start(u32[32]{0:T(128)} %constant.89) | copy-start | bytes 388
  0.0 14.6 %copy-start = (bf16[128,3456]{1,0:T(8,128)(2,1)S(1)}, bf16[128,3456]{1,0:T(8,128)(2,1)}, u32[]{:S(2)}) copy-start(bf16[128,3456]{1,0:T(8,128)(2,1)} %param.7) | copy-start | bytes 2654212
  0.0 8.3 %copy-start.1 = (bf16[128,5120]{1,0:T(8,128)(2,1)S(1)}, bf16[128,5120]{1,0:T(8,128)(2,1)}, u32[]{:S(2)}) copy-start(bf16[128,5120]{1,0:T(8,128)(2,1)} %param.8) | copy-start | bytes 3932164
  9.7 26.4 %all-to-all-start = ((bf16[128,2,2560]{2,0,1:T(8,128)(2,1)}), bf16[128,2,2560]{2,0,1:T(8,128)(2,1)S(1)}, u32[]{:S(2)}, u32[]{:S(2)}) async-start(bf16[128,2,2560]{2,0,1:T(8,128)(2,1)} %bitcast.31), calls=%async_computation | async-start | bytes 2621440 | tf_op jit(solution)/shard_map/all_to_all | solution.py:23
  49.2 659.6 %copy-start.2 = (s32[4]{0:T(128)S(1)}, s32[4]{0:T(128)}, u32[]{:S(2)}) copy-start(s32[4]{0:T(128)} %param.11) | copy-start | bytes 52
  49.2 194.4 %collective-permute-start = (f32[1,864,2560]{2,1,0:T(8,128)}, f32[1,864,2560]{2,1,0:T(8,128)}, u32[]{:S(2)}, u32[]{:S(2)}) collective-permute-start(f32[1,864,2560]{2,1,0:T(8,128)} %get-tuple-element.223), channel_id=1, source_target_pairs={{0,4},{4,8},{8,12},{12,0},{1,5},{5,9},{9,13},{13,1},{2,6},{6,10},{... | collective-permute-start | bytes 26542088 | tf_op jit(solution)/shard_map/while/body/eval_jaxpr/ppermute | solution.py:10
  266.0 194.1 %collective-permute-start = (f32[1,864,2560]{2,1,0:T(8,128)}, f32[1,864,2560]{2,1,0:T(8,128)}, u32[]{:S(2)}, u32[]{:S(2)}) collective-permute-start(f32[1,864,2560]{2,1,0:T(8,128)} %get-tuple-element.223), channel_id=1, source_target_pairs={{0,4},{4,8},{8,12},{12,0},{1,5},{5,9},{9,13},{13,1},{2,6},{6,10},{... | collective-permute-start | bytes 26542088 | tf_op jit(solution)/shard_map/while/body/eval_jaxpr/ppermute | solution.py:10
  482.5 194.1 %collective-permute-start = (f32[1,864,2560]{2,1,0:T(8,128)}, f32[1,864,2560]{2,1,0:T(8,128)}, u32[]{:S(2)}, u32[]{:S(2)}) collective-permute-start(f32[1,864,2560]{2,1,0:T(8,128)} %get-tuple-element.223), channel_id=1, source_target_pairs={{0,4},{4,8},{8,12},{12,0},{1,5},{5,9},{9,13},{13,1},{2,6},{6,10},{... | collective-permute-start | bytes 26542088 | tf_op jit(solution)/shard_map/while/body/eval_jaxpr/ppermute | solution.py:10
where the time goes:
time: 710 us; the launch traced here: 709 us
  waiting for transfers between devices  557 us (78%)
  blocking collectives  79 us (11%)
  local copies, waits for them, and re-layouts  34 us (5%)
  matrix products  26.5 us (4%)
    ppermute x3, waiting for transfers between devices, shifted(): return lax.ppermute(value, axis, pairs)  557 us
    all_gather x4, blocking collectives, panel_score(): lax.all_gather(columns, 'seq', axis=0, tiled=True)  45 us
    dot_general x4, matrix products, panel_score(): lax.dot_general(lax.all_gather(columns, 'seq', axis=0, tiled=True), delta...  26.5 us
    psum x4, blocking collectives, add_score(): return running + lax.psum(partial_value, ('seq', 'col'))  25.7 us
    while x3, local copies, waits for them, and re-layouts  22.5 us
  transfers between devices with their start and end apart: 4, of which 3 were waited for; matrix products, arithmetic and copies ran while one was open for 0% of the time, Pallas kernels for 0%

commit v1 on v0

v1 whole, which is shorter than its diff:
```python
import functools

import jax
import jax.numpy as jnp
from jax import lax
from jax.experimental import pallas as pl
from jax.experimental.pallas import tpu as pltpu
from jax.sharding import PartitionSpec as P

MESH = pl.DeviceIdType.MESH


def score_kernel(
    nb, ns, nc,
    a_ref, g_ref, q_ref, assign_ref, out_ref,
    g_all, a_all, q_vmem, part, mine, others,
    local_sem, g_recv, g_right, g_left, g_side, g_x,
    a_recv, a_z, a_x, p_send, p_recv,
):
    b = lax.axis_index("blk")
    s = lax.axis_index("seq")
    c = lax.axis_index("col")
    rows = g_ref.shape[0]
    share = rows // nc
    fp, dl = q_ref.shape[1], q_ref.shape[2]
    my_rows = pl.multiple_of(c * share, share)
    n_dev = nb * ns * nc

    def device(db, ds, dc):
        return {
            "blk": lax.rem(b + db, nb),
            "seq": lax.rem(s + ds, ns),
            "col": lax.rem(c + dc, nc),
        }

    def offsets(t):
        return t // (ns * nc), lax.rem(t // nc, ns), lax.rem(t, nc)

    barrier = pltpu.get_barrier_semaphore()

    @pl.loop(1, n_dev)
    def _(t):
        pl.semaphore_signal(barrier, inc=1, device_id=device(*offsets(t)), device_id_type=MESH)

    def g_rows(tb, cc):
        return pl.ds(pl.multiple_of(tb * rows + cc * share, share), share)

    def g_copy(src, doc, tb, sem, to):
        return pltpu.make_async_remote_copy(
            src_ref=src,
            dst_ref=g_all.at[doc, g_rows(tb, c)],
            send_sem=sem,
            recv_sem=g_recv.at[doc, tb, c],
            device_id=to,
            device_id_type=MESH,
        )

    def g_landed(doc, tb, cc):
        pltpu.make_async_copy(
            g_all.at[doc, g_rows(tb, cc)], g_all.at[doc, g_rows(tb, cc)], g_recv.at[doc, tb, cc]
        ).wait()

    def own_columns(tb):
        return g_ref.at[pl.ds(my_rows, share), pl.ds(pl.multiple_of(tb * dl, 128), dl)]

    def right_copy(src, doc, tb):
        return g_copy(src, doc, tb, g_right.at[doc, tb], {"blk": b + 1})

    def left_copy(src, doc, tb):
        return g_copy(src, doc, tb, g_left.at[doc, tb], {"blk": b - 1})

    def side_copy(doc, tb):
        return g_copy(
            g_all.at[doc, g_rows(tb, c)], doc, tb, g_side.at[doc, tb], device(0, 0, 1)
        )

    def x_copy(ds):
        return g_copy(own_columns(lax.rem(s + ds, ns)), b, s, g_x.at[ds - 1], device(0, ds, 0))

    def a_z_copy(db):
        to = lax.rem(b + db, nb)
        return pltpu.make_async_remote_copy(
            src_ref=a_ref.at[to],
            dst_ref=a_all.at[b, s],
            send_sem=a_z.at[db - 1],
            recv_sem=a_recv.at[b, s],
            device_id={"blk": to},
            device_id_type=MESH,
        )

    def a_x_copy(src, doc, ds):
        return pltpu.make_async_remote_copy(
            src_ref=src,
            dst_ref=a_all.at[doc, s],
            send_sem=a_x.at[doc, ds - 1],
            recv_sem=a_recv.at[doc, s],
            device_id=device(0, ds, 0),
            device_id_type=MESH,
        )

    def a_landed(doc, tb):
        pltpu.make_async_copy(a_all.at[doc, tb], a_all.at[doc, tb], a_recv.at[doc, tb]).wait()

    q_copy = pltpu.make_async_copy(q_ref.at[0], q_vmem, local_sem.at[0])
    own_g_copy = pltpu.make_async_copy(
        g_ref.at[:, pl.ds(pl.multiple_of(s * dl, 128), dl)],
        g_all.at[b, pl.ds(pl.multiple_of(s * rows, rows), rows)],
        local_sem.at[1],
    )
    own_a_copy = pltpu.make_async_copy(a_ref.at[b], a_all.at[b, s], local_sem.at[2])
    own_g_copy.start()
    own_a_copy.start()
    q_copy.start()

    pl.semaphore_wait(barrier, n_dev - 1)

    for ds in range(1, ns):
        x_copy(ds).start()

    @pl.when(b < nb - 1)
    def _():
        right_copy(own_columns(s), b, s).start()

    @pl.when(b > 0)
    def _():
        left_copy(own_columns(s), b, s).start()

    for db in range(1, nb):
        a_z_copy(db).start()
    for ds in range(1, ns):
        a_x_copy(a_ref.at[b], b, ds).start()

    def score(doc):
        for ds in range(1, ns):
            a_landed(doc, lax.rem(s + ds, ns))
        lhs = jnp.concatenate([a_all[doc, tb] for tb in range(ns)], axis=1)
        tile = 256 if dl % 256 == 0 else 128

        def one_tile(i, acc):
            columns = pl.ds(pl.multiple_of(i * tile, tile), tile)
            grad = jnp.dot(lhs, g_all[doc, :, columns], preferred_element_type=jnp.float32)
            prod = grad * q_vmem[:, columns]
            return acc + jnp.sum(prod.reshape(fp // 8, 8, tile), axis=0)

        acc = lax.fori_loop(0, dl // tile, one_tile, jnp.zeros((8, tile), jnp.float32))
        part[doc] = sum(acc[:, i * 128:(i + 1) * 128] for i in range(tile // 128))

    for ds in range(1, ns):
        tb = lax.rem(s + ds, ns)
        g_landed(b, tb, c)
        src = g_all.at[b, g_rows(tb, c)]

        @pl.when(b < nb - 1)
        def _():
            right_copy(src, b, tb).start()

        @pl.when(b > 0)
        def _():
            left_copy(src, b, tb).start()

        side_copy(b, tb).start()

    def relay(doc, onward, may_go_on):
        a_landed(doc, s)
        for ds in range(1, ns):
            a_x_copy(a_all.at[doc, s], doc, ds).start()
        for ds in range(ns):
            tb = lax.rem(s + ds, ns)
            g_landed(doc, tb, c)

            @pl.when(may_go_on)
            def _():
                onward(g_all.at[doc, g_rows(tb, c)], doc, tb).start()

            side_copy(doc, tb).start()

    def score_far(doc):
        for tb in range(ns):
            g_landed(doc, tb, 1 - c)
        score(doc)

    def from_left(k, act):
        @pl.when(b - k >= 0)
        def _():
            act(b - k)

    def from_right(k, act):
        @pl.when(b + k < nb)
        def _():
            act(b + k)

    def score_own():
        own_a_copy.wait()
        own_g_copy.wait()
        q_copy.wait()
        for ds in range(1, ns):
            g_landed(b, lax.rem(s + ds, ns), 1 - c)
        score(b)

    for k in range(1, nb):
        from_left(k, lambda doc: relay(doc, right_copy, b < nb - 1))
        from_right(k, lambda doc: relay(doc, left_copy, b > 0))
        if k == 1:
            score_own()
        else:
            from_left(k - 1, score_far)
            from_right(k - 1, score_far)
    from_left(nb - 1, score_far)
    from_right(nb - 1, score_far)

    mine[...] = jnp.concatenate([jnp.sum(part[j], axis=0, keepdims=True) for j in range(nb)], axis=0)

    def p_copy(t):
        return pltpu.make_async_remote_copy(
            src_ref=mine,
            dst_ref=others.at[t],
            send_sem=p_send.at[t],
            recv_sem=p_recv.at[t],
            device_id=device(*offsets(t)),
            device_id_type=MESH,
        )

    @pl.loop(1, n_dev)
    def _(t):
        p_copy(t).start()

    for ds in range(1, ns):
        x_copy(ds).wait_send()
        a_x_copy(a_ref.at[b], b, ds).wait_send()
    for db in range(1, nb):
        a_z_copy(db).wait_send()

    @pl.when(b < nb - 1)
    def _():
        right_copy(own_columns(s), b, s).wait_send()

    @pl.when(b > 0)
    def _():
        left_copy(own_columns(s), b, s).wait_send()

    for ds in range(1, ns):
        tb = lax.rem(s + ds, ns)
        src = g_all.at[b, g_rows(tb, c)]

        @pl.when(b < nb - 1)
        def _():
            right_copy(src, b, tb).wait_send()

        @pl.when(b > 0)
        def _():
            left_copy(src, b, tb).wait_send()

        side_copy(b, tb).wait_send()

    def relay_sent(doc, onward, may_go_on):
        for ds in range(1, ns):
            a_x_copy(a_all.at[doc, s], doc, ds).wait_send()
        for ds in range(ns):
            tb = lax.rem(s + ds, ns)

            @pl.when(may_go_on)
            def _():
                onward(g_all.at[doc, g_rows(tb, c)], doc, tb).wait_send()

            side_copy(doc, tb).wait_send()

    for k in range(1, nb):
        from_left(k, lambda doc: relay_sent(doc, right_copy, b < nb - 1))
        from_right(k, lambda doc: relay_sent(doc, left_copy, b > 0))

    @pl.loop(1, n_dev)
    def _(t):
        p_copy(t).wait()

    def add_one(t, total):
        return total + others[t]

    total = lax.fori_loop(1, n_dev, add_one, mine[...])
    chosen = jnp.zeros((1, 128), jnp.float32)
    for j in range(nb):
        chosen = chosen + jnp.where(assign_ref[j] == b, total[j:j + 1], 0.0)
    out_ref[...] = jnp.sum(chosen, axis=1, keepdims=True)


def on_device(activations, output_grads, queries, lengths, assignment):
    nb, ns, nc = lax.axis_size("blk"), lax.axis_size("seq"), lax.axis_size("col")
    rows, d_model = output_grads.shape
    fp, dl = queries.shape[1], queries.shape[2]
    positions = lax.axis_index("seq") * rows + jnp.arange(rows, dtype=jnp.int32)
    masked = jnp.where((positions < lengths[0])[:, None], activations, jnp.zeros_like(activations))
    panels = masked.reshape(rows, nb, fp).transpose(1, 2, 0)
    n_dev = nb * ns * nc
    dma = pltpu.SemaphoreType.DMA
    return pl.pallas_call(
        functools.partial(score_kernel, nb, ns, nc),
        out_shape=jax.ShapeDtypeStruct((1, 1), jnp.float32),
        in_specs=[
            pl.BlockSpec(memory_space=pl.ANY),
            pl.BlockSpec(memory_space=pl.ANY),
            pl.BlockSpec(memory_space=pl.ANY),
            pl.BlockSpec(memory_space=pltpu.SMEM),
        ],
        out_specs=pl.BlockSpec(memory_space=pltpu.VMEM),
        scratch_shapes=[
            pltpu.VMEM((nb, ns * rows, dl), jnp.bfloat16),
            pltpu.VMEM((nb, ns, fp, rows), jnp.bfloat16),
            pltpu.VMEM((fp, dl), jnp.float32),
            pltpu.VMEM((nb, 8, 128), jnp.float32),
            pltpu.VMEM((nb, 128), jnp.float32),
            pltpu.VMEM((n_dev, nb, 128), jnp.float32),
            dma((3,)),
            dma((nb, ns, nc)),
            dma((nb, ns)),
            dma((nb, ns)),
            dma((nb, ns)),
            dma((max(ns - 1, 1),)),
            dma((nb, ns)),
            dma((max(nb - 1, 1),)),
            dma((nb, max(ns - 1, 1))),
            dma((n_dev,)),
            dma((n_dev,)),
        ],
        compiler_params=pltpu.CompilerParams(
            collective_id=0, has_side_effects=True, vmem_limit_bytes=56 * 1024 * 1024
        ),
        cost_estimate=pl.CostEstimate(
            flops=2 * nb * ns * rows * fp * dl, bytes_accessed=4 * fp * dl, transcendentals=0
        ),
    )(panels, output_grads, queries, assignment)


def solution(mesh):
    in_specs = (
        P(("grp", "blk", "seq"), "col"),
        P(("grp", "blk", "seq"), None),
        P("grp", ("col", "blk"), "seq"),
        P(("grp", "blk")),
        P("grp"),
    )
    out_specs = P(None, ("grp", "blk"))
    return jax.shard_map(
        on_device, mesh=mesh, in_specs=in_specs, out_specs=out_specs, check_vma=False
    )
```

time: 710 us -> 82.2 us (0.12)
  waiting for transfers between devices: 557 us -> 0 us
  blocking collectives: 79 us -> 0 us
  Pallas kernels: 0 us -> 77.6 us
  local copies, waits for them, and re-layouts: 34 us -> 1.33 us
  matrix products: 26.5 us -> 0 us
    ppermute x3 -> x0, waiting for transfers between devices: 557 us -> none  [shifted(): return lax.ppermute(value, axis, pairs)]
    pallas_call x0 -> x1, Pallas kernels: none -> 77.6 us  [on_device(): pl.pallas_call(functools.partial(score_kernel, nb, ns, nc), out_shape=jax...]
    all_gather x4 -> x0, blocking collectives: 45 us -> none  [panel_score(): lax.all_gather(columns, 'seq', axis=0, tiled=True)]
    dot_general x4 -> x0, matrix products: 26.5 us -> none  [panel_score(): lax.dot_general(lax.all_gather(columns, 'seq', axis=0, tiled=True), delta...]
    psum x4 -> x0, blocking collectives: 25.7 us -> none  [add_score(): return running + lax.psum(partial_value, ('seq', 'col'))]
    while x3 -> x0, local copies, waits for them, and re-layouts: 22.5 us -> none
    unnamed x12 -> x0, local copies, waits for them, and re-layouts: 9.77 us -> none
    unnamed x1 -> x0, blocking collectives: 8.34 us -> none
  transfers between devices with their start and end apart: 4 -> 0, of which waited for: 3 -> 0; matrix products, arithmetic and copies ran while one was open for 0% -> 0% of each run, Pallas kernels for 0% -> 0%
where the time goes in v1:
time: 82.2 us; the launch traced here: 82 us
  Pallas kernels  77.6 us (94%)
  between operations  1.74 us (2%)
  other arithmetic  1.33 us (2%)
  local copies, waits for them, and re-layouts  1.33 us (2%)
    pallas_call x1, Pallas kernels, on_device(): pl.pallas_call(functools.partial(score_kernel, nb, ns, nc), out_shape=jax...  77.6 us

profile of v1, /device:TPU:0, one launch (start us, length us, event | category | flops | bytes accessed | tf_op | source)
XLA Modules:
  0.0 82.0 jit_solution(13456270592009010085)
XLA Ops:
  0.7 1.3 %broadcast_select_fusion = bf16[128,3456]{1,0:T(8,128)(2,1)S(1)} fusion(bf16[128,3456]{1,0:T(8,128)(2,1)} %param.5, pred[128]{0:T(512)(128)(4,1)S(1)} %add_compare_fusion), kind=kLoop, calls=%fused_computation | loop fusion | flops 442368 | bytes 1769600 | tf_op jit(solution)/shard_map/jit(_where)/select_n | solution.py:290
  2.0 1.3 %copy.6 = bf16[128,3456]{0,1:T(8,128)(2,1)} copy(bf16[128,3456]{1,0:T(8,128)(2,1)S(1)} %broadcast_select_fusion) | data formatting | bytes 1769472 | tf_op jit(solution)/shard_map/jit(_where)/select_n | solution.py:290
  3.3 77.6 %shard_map.55 = f32[1,1]{1,0:T(1,128)} custom-call(bf16[4,864,128]{2,1,0:T(8,128)(2,1)} %bitcast.5, bf16[128,5120]{1,0:T(8,128)(2,1)} %g_ref.1, f32[1,864,2560]{2,1,0:T(8,128)} %q_ref.1, s32[4]{0:T(128)} %assign_ref.1), custom_call_target="tpu_custom_call" | custom-call | flops 4529848320 | bytes 8847360 | tf_op jit(solution)/shard_map/pallas_call | solution.py:294
  (1 shorter events, 0.0 us)

commit v2 on v1

v2 whole, which is shorter than its diff:
```python
import functools

import jax
import jax.numpy as jnp
from jax import lax
from jax.experimental import pallas as pl
from jax.experimental.pallas import tpu as pltpu
from jax.sharding import PartitionSpec as P

MESH = pl.DeviceIdType.MESH


def score_kernel(
    nb, ns, nc,
    a_ref, g_ref, q_ref, length_ref, assign_ref, out_ref,
    g_all, a_all, a_own, a_panels, q_vmem, q_high, q_low, a_doc, y_doc,
    y_out, y_in, y_sum, y_far, part, mine, others,
    local_sem, g_recv, g_right, g_left, g_side, g_x,
    a_recv, a_z, a_x, y_send, y_recv, p_send, p_recv,
):
    b = lax.axis_index("blk")
    s = lax.axis_index("seq")
    c = lax.axis_index("col")
    rows = g_ref.shape[0]
    share = rows // nc
    fp, dl = q_vmem.shape
    tile = next(t for t in (512, 256, 128) if dl % t == 0)
    my_rows = pl.multiple_of(c * share, share)
    n_dev = nb * ns * nc

    def device(db, ds, dc):
        return {
            "blk": lax.rem(b + db, nb),
            "seq": lax.rem(s + ds, ns),
            "col": lax.rem(c + dc, nc),
        }

    def offsets(t):
        return t // (ns * nc), lax.rem(t // nc, ns), lax.rem(t, nc)

    barrier = pltpu.get_barrier_semaphore()

    @pl.loop(1, n_dev)
    def _(t):
        pl.semaphore_signal(barrier, inc=1, device_id=device(*offsets(t)), device_id_type=MESH)

    a_copy = pltpu.make_async_copy(a_ref, a_own, local_sem.at[2])
    q_copy = pltpu.make_async_copy(q_ref.at[0], q_vmem, local_sem.at[0])
    own_g_copy = pltpu.make_async_copy(
        g_ref.at[:, pl.ds(pl.multiple_of(s * dl, 128), dl)],
        g_all.at[b, pl.ds(pl.multiple_of(s * rows, rows), rows)],
        local_sem.at[1],
    )
    a_copy.start()
    own_g_copy.start()
    q_copy.start()

    def g_rows(tb, cc):
        return pl.ds(pl.multiple_of(tb * rows + cc * share, share), share)

    def g_copy(src, doc, tb, sem, to):
        return pltpu.make_async_remote_copy(
            src_ref=src,
            dst_ref=g_all.at[doc, g_rows(tb, c)],
            send_sem=sem,
            recv_sem=g_recv.at[doc, tb, c],
            device_id=to,
            device_id_type=MESH,
        )

    def g_landed(doc, tb, cc):
        pltpu.make_async_copy(
            g_all.at[doc, g_rows(tb, cc)], g_all.at[doc, g_rows(tb, cc)], g_recv.at[doc, tb, cc]
        ).wait()

    def own_columns(tb):
        return g_ref.at[pl.ds(my_rows, share), pl.ds(pl.multiple_of(tb * dl, 128), dl)]

    def right_copy(src, doc, tb):
        return g_copy(src, doc, tb, g_right.at[doc, tb], {"blk": b + 1})

    def left_copy(src, doc, tb):
        return g_copy(src, doc, tb, g_left.at[doc, tb], {"blk": b - 1})

    def side_copy(doc, tb):
        return g_copy(
            g_all.at[doc, g_rows(tb, c)], doc, tb, g_side.at[doc, tb], device(0, 0, 1)
        )

    def x_copy(ds):
        return g_copy(own_columns(lax.rem(s + ds, ns)), b, s, g_x.at[ds - 1], device(0, ds, 0))

    def a_z_copy(db):
        to = lax.rem(b + db, nb)
        return pltpu.make_async_remote_copy(
            src_ref=a_panels.at[to],
            dst_ref=a_all.at[b, s],
            send_sem=a_z.at[db - 1],
            recv_sem=a_recv.at[b, s],
            device_id={"blk": to},
            device_id_type=MESH,
        )

    def a_x_copy(src, doc, ds):
        return pltpu.make_async_remote_copy(
            src_ref=src,
            dst_ref=a_all.at[doc, s],
            send_sem=a_x.at[doc, ds - 1],
            recv_sem=a_recv.at[doc, s],
            device_id=device(0, ds, 0),
            device_id_type=MESH,
        )

    def a_landed(doc, tb):
        pltpu.make_async_copy(a_all.at[doc, tb], a_all.at[doc, tb], a_recv.at[doc, tb]).wait()

    y_side_copy = pltpu.make_async_remote_copy(
        src_ref=y_out.at[pl.ds(pl.multiple_of((1 - c) * share, share), share)],
        dst_ref=y_in,
        send_sem=y_send.at[0],
        recv_sem=y_recv.at[2],
        device_id=device(0, 0, 1),
        device_id_type=MESH,
    )

    def y_z_copy(side, to):
        return pltpu.make_async_remote_copy(
            src_ref=y_sum,
            dst_ref=y_far.at[side],
            send_sem=y_send.at[1],
            recv_sem=y_recv.at[side],
            device_id={"blk": to},
            device_id_type=MESH,
        )

    positions = s * rows + lax.broadcasted_iota(jnp.int32, (rows, 1), 0)
    valid = jnp.where(positions < length_ref[0], 1.0, 0.0).astype(jnp.bfloat16)
    a_copy.wait()
    for p in range(nb):
        a_panels[p] = (a_own[:, p * fp:(p + 1) * fp] * valid).T

    pl.semaphore_wait(barrier, n_dev - 1)

    for db in range(1, nb):
        a_z_copy(db).start()
    for ds in range(1, ns):
        x_copy(ds).start()

    @pl.when(b < nb - 2)
    def _():
        right_copy(own_columns(s), b, s).start()

    @pl.when(b > 1)
    def _():
        left_copy(own_columns(s), b, s).start()

    for ds in range(1, ns):
        a_x_copy(a_panels.at[b], b, ds).start()

    part[...] = jnp.zeros_like(part)
    q_copy.wait()
    step_rows = next(t for t in (96, 72, 8) if fp % t == 0)

    @pl.loop(0, fp // step_rows)
    def _(i):
        here = pl.ds(pl.multiple_of(i * step_rows, step_rows), step_rows)
        value = q_vmem[here, :]
        high = value.astype(jnp.bfloat16)
        q_high[here, :] = high
        q_low[here, :] = (value - high.astype(jnp.float32)).astype(jnp.bfloat16)

    def a_relay(doc):
        a_landed(doc, s)
        for ds in range(1, ns):
            a_x_copy(a_all.at[doc, s], doc, ds).start()

    def products(a_rows, store):
        @pl.loop(0, dl // tile)
        def _(i):
            columns = pl.ds(pl.multiple_of(i * tile, tile), tile)
            store(
                columns,
                jnp.dot(a_rows[...], q_high[:, columns], preferred_element_type=jnp.float32)
                + jnp.dot(a_rows[...], q_low[:, columns], preferred_element_type=jnp.float32),
            )

    def doc_products(doc, slot, own):
        for tb in range(ns):
            def take(ref):
                a_doc[tb * rows:(tb + 1) * rows, :] = ref[...].T

            if own:
                @pl.when(tb == s)
                def _():
                    take(a_panels.at[doc])

                @pl.when(tb != s)
                def _():
                    a_landed(doc, tb)
                    take(a_all.at[doc, tb])
            else:
                @pl.when(tb != s)
                def _():
                    a_landed(doc, tb)

                take(a_all.at[doc, tb])

        def store(columns, value):
            y_doc[slot, :, columns] = value

        products(a_doc, store)

    def add_product(doc, y, g):
        count = y.shape[0]

        def one_tile(i, acc):
            columns = pl.ds(pl.multiple_of(i * tile, tile), tile)
            prod = y[:, columns] * g[:, columns].astype(jnp.float32)
            return acc + jnp.sum(prod.reshape(count // 8, 8, tile), axis=0)

        acc = lax.fori_loop(0, dl // tile, one_tile, jnp.zeros((8, tile), jnp.float32))
        part[doc] += sum(acc[:, i * 128:(i + 1) * 128] for i in range(tile // 128))

    def add_block(doc, slot, tb):
        here = pl.ds(pl.multiple_of(tb * rows, rows), rows)
        add_product(doc, y_doc.at[slot, here], g_all.at[doc, here])

    def from_left(k, act):
        @pl.when(b - k >= 0)
        def _():
            act(b - k)

    def from_right(k, act):
        @pl.when(b + k < nb)
        def _():
            act(b + k)

    at_right_end = b == nb - 1
    at_left_end = b == 0

    from_left(1, a_relay)
    from_right(1, a_relay)

    def give_products(doc, side):
        a_doc[0:rows, :] = a_all[doc, s].T

        def store(columns, value):
            y_out[:, columns] = value

        products(a_doc.at[0:rows], store)
        y_side_copy.start()
        y_side_copy.wait_recv()
        y_sum[...] = y_out[pl.ds(my_rows, share), :] + y_in[...]
        y_z_copy(side, doc).start()

    @pl.when(at_left_end)
    def _():
        give_products(b + 1, 0)

    @pl.when(at_right_end)
    def _():
        give_products(b - 1, 1)

    for ds in range(1, ns):
        tb = lax.rem(s + ds, ns)
        g_landed(b, tb, c)
        src = g_all.at[b, g_rows(tb, c)]

        @pl.when(b < nb - 1)
        def _():
            right_copy(src, b, tb).start()

        @pl.when(b > 0)
        def _():
            left_copy(src, b, tb).start()

        side_copy(b, tb).start()

    def relay(doc, tb, onward, may_go_on):
        g_landed(doc, tb, c)

        @pl.when(may_go_on)
        def _():
            onward(g_all.at[doc, g_rows(tb, c)], doc, tb).start()

        side_copy(doc, tb).start()

    def add_far(doc, slot, tb):
        g_landed(doc, tb, 1 - c)
        add_block(doc, slot, tb)

    def sides(k, ds):
        left, right = b - k >= 0, b + k < nb
        if k == 1 and ds == 0:
            left, right = left & (b < nb - 1), right & (b > 0)
        return left, right

    doc_products(b, 0, True)
    own_g_copy.wait()
    add_block(b, 0, s)
    for ds in range(1, ns):
        tb = lax.rem(s + ds, ns)
        g_landed(b, tb, 1 - c)
        add_block(b, 0, tb)

    for k in range(1, nb):
        if k + 1 < nb:
            from_left(k + 1, a_relay)
            from_right(k + 1, a_relay)
        from_left(k, lambda doc: doc_products(doc, 0, False))
        from_right(k, lambda doc: doc_products(doc, 1, False))
        for ds in range(ns):
            tb = lax.rem(s + ds, ns)
            left, right = sides(k, ds)

            @pl.when(left)
            def _():
                relay(b - k, tb, right_copy, b < nb - 1)

            @pl.when(right)
            def _():
                relay(b + k, tb, left_copy, b > 0)

            @pl.when(left)
            def _():
                add_far(b - k, 0, tb)

            @pl.when(right)
            def _():
                add_far(b + k, 1, tb)

        if k == 1:
            own_here = g_all.at[b, g_rows(s, c)]

            def take_products(side):
                y_z_copy(side, b).wait_recv()
                add_product(b, y_far.at[side], own_here)

            @pl.when(b == 1)
            def _():
                take_products(0)

            @pl.when(b == nb - 2)
            def _():
                take_products(1)

    mine[...] = jnp.concatenate([jnp.sum(part[j], axis=0, keepdims=True) for j in range(nb)], axis=0)

    def p_copy(t):
        return pltpu.make_async_remote_copy(
            src_ref=mine,
            dst_ref=others.at[t],
            send_sem=p_send.at[t],
            recv_sem=p_recv.at[t],
            device_id=device(*offsets(t)),
            device_id_type=MESH,
        )

    @pl.loop(1, n_dev)
    def _(t):
        p_copy(t).start()

    for ds in range(1, ns):
        x_copy(ds).wait_send()
        a_x_copy(a_panels.at[b], b, ds).wait_send()
    for db in range(1, nb):
        a_z_copy(db).wait_send()

    @pl.when(at_left_end)
    def _():
        y_side_copy.wait_send()
        y_z_copy(0, b + 1).wait_send()

    @pl.when(at_right_end)
    def _():
        y_side_copy.wait_send()
        y_z_copy(1, b - 1).wait_send()

    @pl.when(b < nb - 2)
    def _():
        right_copy(own_columns(s), b, s).wait_send()

    @pl.when(b > 1)
    def _():
        left_copy(own_columns(s), b, s).wait_send()

    for ds in range(1, ns):
        tb = lax.rem(s + ds, ns)
        src = g_all.at[b, g_rows(tb, c)]

        @pl.when(b < nb - 1)
        def _():
            right_copy(src, b, tb).wait_send()

        @pl.when(b > 0)
        def _():
            left_copy(src, b, tb).wait_send()

        side_copy(b, tb).wait_send()

    def a_relay_sent(doc):
        for ds in range(1, ns):
            a_x_copy(a_all.at[doc, s], doc, ds).wait_send()

    def relay_sent(doc, tb, onward, may_go_on):
        @pl.when(may_go_on)
        def _():
            onward(g_all.at[doc, g_rows(tb, c)], doc, tb).wait_send()

        side_copy(doc, tb).wait_send()

    for k in range(1, nb):
        from_left(k, a_relay_sent)
        from_right(k, a_relay_sent)
        for ds in range(ns):
            tb = lax.rem(s + ds, ns)
            left, right = sides(k, ds)

            @pl.when(left)
            def _():
                relay_sent(b - k, tb, right_copy, b < nb - 1)

            @pl.when(right)
            def _():
                relay_sent(b + k, tb, left_copy, b > 0)

    @pl.loop(1, n_dev)
    def _(t):
        p_copy(t).wait()

    def add_one(t, total):
        return total + others[t]

    total = lax.fori_loop(1, n_dev, add_one, mine[...])
    chosen = jnp.zeros((1, 128), jnp.float32)
    for j in range(nb):
        chosen = chosen + jnp.where(assign_ref[j] == b, total[j:j + 1], 0.0)
    out_ref[...] = jnp.sum(chosen, axis=1, keepdims=True)


def on_device(activations, output_grads, queries, lengths, assignment):
    nb, ns, nc = lax.axis_size("blk"), lax.axis_size("seq"), lax.axis_size("col")
    rows = output_grads.shape[0]
    fp, dl = queries.shape[1], queries.shape[2]
    n_dev = nb * ns * nc
    dma = pltpu.SemaphoreType.DMA
    return pl.pallas_call(
        functools.partial(score_kernel, nb, ns, nc),
        out_shape=jax.ShapeDtypeStruct((1, 1), jnp.float32),
        in_specs=[
            pl.BlockSpec(memory_space=pl.ANY),
            pl.BlockSpec(memory_space=pl.ANY),
            pl.BlockSpec(memory_space=pl.ANY),
            pl.BlockSpec(memory_space=pltpu.SMEM),
            pl.BlockSpec(memory_space=pltpu.SMEM),
        ],
        out_specs=pl.BlockSpec(memory_space=pltpu.VMEM),
        scratch_shapes=[
            pltpu.VMEM((nb, ns * rows, dl), jnp.bfloat16),
            pltpu.VMEM((nb, ns, fp, rows), jnp.bfloat16),
            pltpu.VMEM((rows, nb * fp), jnp.bfloat16),
            pltpu.VMEM((nb, fp, rows), jnp.bfloat16),
            pltpu.VMEM((fp, dl), jnp.float32),
            pltpu.VMEM((fp, dl), jnp.bfloat16),
            pltpu.VMEM((fp, dl), jnp.bfloat16),
            pltpu.VMEM((ns * rows, fp), jnp.bfloat16),
            pltpu.VMEM((2, ns * rows, dl), jnp.float32),
            pltpu.VMEM((rows, dl), jnp.float32),
            pltpu.VMEM((rows // nc, dl), jnp.float32),
            pltpu.VMEM((rows // nc, dl), jnp.float32),
            pltpu.VMEM((2, rows // nc, dl), jnp.float32),
            pltpu.VMEM((nb, 8, 128), jnp.float32),
            pltpu.VMEM((nb, 128), jnp.float32),
            pltpu.VMEM((n_dev, nb, 128), jnp.float32),
            dma((3,)),
            dma((nb, ns, nc)),
            dma((nb, ns)),
            dma((nb, ns)),
            dma((nb, ns)),
            dma((max(ns - 1, 1),)),
            dma((nb, ns)),
            dma((max(nb - 1, 1),)),
            dma((nb, max(ns - 1, 1))),
            dma((2,)),
            dma((3,)),
            dma((n_dev,)),
            dma((n_dev,)),
        ],
        compiler_params=pltpu.CompilerParams(
            collective_id=0, has_side_effects=True, vmem_limit_bytes=56 * 1024 * 1024
        ),
        cost_estimate=pl.CostEstimate(
            flops=2 * nb * ns * rows * fp * dl, bytes_accessed=4 * fp * dl, transcendentals=0
        ),
    )(activations, output_grads, queries, lengths, assignment)


def solution(mesh):
    in_specs = (
        P(("grp", "blk", "seq"), "col"),
        P(("grp", "blk", "seq"), None),
        P("grp", ("col", "blk"), "seq"),
        P(("grp", "blk")),
        P("grp"),
    )
    out_specs = P(None, ("grp", "blk"))
    return jax.shard_map(
        on_device, mesh=mesh, in_specs=in_specs, out_specs=out_specs, check_vma=False
    )
```

time: 82.2 us -> 81.2 us (0.988)
  Pallas kernels: 77.6 us -> 79.2 us
  other arithmetic: 1.33 us -> 0 us
  local copies, waits for them, and re-layouts: 1.33 us -> 0 us
    pallas_call x1, Pallas kernels: 77.6 us -> 79.2 us  [on_device(): pl.pallas_call(functools.partial(score_kernel, nb, ns, nc), out_shape=jax...]
    select_n x1 -> x0, local copies, waits for them, and re-layouts: 1.33 us -> none  [on_device(): jnp.where((positions < lengths[0])[:, None], activations, jnp.zeros_like(...]
    select_n x1 -> x0, other arithmetic: 1.32 us -> none  [on_device(): jnp.where((positions < lengths[0])[:, None], activations, jnp.zeros_like(...]
where the time goes in v2:
time: 81.2 us; the launch traced here: 81 us
  Pallas kernels  79.2 us (98%)
  between operations  1.85 us (2%)
    pallas_call x1, Pallas kernels, on_device(): pl.pallas_call(functools.partial(score_kernel, nb, ns, nc), out_shape=jax...  79.2 us

profile of v2, /device:TPU:0, one launch (start us, length us, event | category | flops | bytes accessed | tf_op | source)
XLA Modules:
  0.0 81.0 jit_solution(5697928053154629077)
XLA Ops:
  0.7 79.2 %shard_map.55 = f32[1,1]{1,0:T(1,128)} custom-call(bf16[128,3456]{1,0:T(8,128)(2,1)} %a_ref.1, bf16[128,5120]{1,0:T(8,128)(2,1)} %g_ref.1, f32[1,864,2560]{2,1,0:T(8,128)} %q_ref.1, s32[1]{0:T(128)S(6)} %copy.7.length_ref, s32[4]{0:T(128)} %assign_ref.1), custom_call_target="tpu_custom_call" | custom-call | flops 4529848320 | bytes 8847360 | tf_op jit(solution)/shard_map/pallas_call | solution.py:447

commit v3 on v2

--- a/solution.py
+++ b/solution.py
@@ -238,9 +238,6 @@
     at_right_end = b == nb - 1
     at_left_end = b == 0
 
-    from_left(1, a_relay)
-    from_right(1, a_relay)
-
     def give_products(doc, side):
         a_doc[0:rows, :] = a_all[doc, s].T
 
@@ -251,15 +248,6 @@
         y_side_copy.start()
         y_side_copy.wait_recv()
         y_sum[...] = y_out[pl.ds(my_rows, share), :] + y_in[...]
-        y_z_copy(side, doc).start()
-
-    @pl.when(at_left_end)
-    def _():
-        give_products(b + 1, 0)
-
-    @pl.when(at_right_end)
-    def _():
-        give_products(b - 1, 1)
 
     for ds in range(1, ns):
         tb = lax.rem(s + ds, ns)
@@ -275,6 +263,11 @@
             left_copy(src, b, tb).start()
 
         side_copy(b, tb).start()
+
+    def a_relays(k):
+        if k < nb:
+            from_left(k, a_relay)
+            from_right(k, a_relay)
 
     def relay(doc, tb, onward, may_go_on):
         g_landed(doc, tb, c)
@@ -294,6 +287,57 @@
         if k == 1 and ds == 0:
             left, right = left & (b < nb - 1), right & (b > 0)
         return left, right
+
+    def relays(k, ds):
+        tb = lax.rem(s + ds, ns)
+        left, right = sides(k, ds)
+
+        @pl.when(left)
+        def _():
+            relay(b - k, tb, right_copy, b < nb - 1)
+
+        @pl.when(right)
+        def _():
+            relay(b + k, tb, left_copy, b > 0)
+
+    def add_blocks(k, ds):
+        tb = lax.rem(s + ds, ns)
+        left, right = sides(k, ds)
+
+        @pl.when(left)
+        def _():
+            add_far(b - k, 0, tb)
+
+        @pl.when(right)
+        def _():
+            add_far(b + k, 1, tb)
+
+    a_relays(1)
+
+    @pl.when(at_left_end)
+    def _():
+        give_products(b + 1, 0)
+
+    @pl.when(at_right_end)
+    def _():
+        give_products(b - 1, 1)
+
+    relays(1, 0)
+    a_relays(2)
+
+    @pl.when(at_left_end)
+    def _():
+        for ds in range(1, ns):
+            tb = lax.rem(s + ds, ns)
+            right_copy(g_all.at[b, g_rows(tb, c)], b, tb).wait_send()
+        y_z_copy(0, b + 1).start()
+
+    @pl.when(at_right_end)
+    def _():
+        for ds in range(1, ns):
+            tb = lax.rem(s + ds, ns)
+            left_copy(g_all.at[b, g_rows(tb, c)], b, tb).wait_send()
+        y_z_copy(1, b - 1).start()
 
     doc_products(b, 0, True)
     own_g_copy.wait()
@@ -304,45 +348,33 @@
         add_block(b, 0, tb)
 
     for k in range(1, nb):
-        if k + 1 < nb:
-            from_left(k + 1, a_relay)
-            from_right(k + 1, a_relay)
-        from_left(k, lambda doc: doc_products(doc, 0, False))
-        from_right(k, lambda doc: doc_products(doc, 1, False))
+        if k > 1:
+            relays(k, 0)
+            a_relays(k + 1)
+        if k > 1:
+            from_left(k, lambda doc: doc_products(doc, 0, False))
+            from_right(k, lambda doc: doc_products(doc, 1, False))
+        for ds in range(1, ns):
+            relays(k, ds)
+        if k == 1:
+            from_left(k, lambda doc: doc_products(doc, 0, False))
+            from_right(k, lambda doc: doc_products(doc, 1, False))
         for ds in range(ns):
-            tb = lax.rem(s + ds, ns)
-            left, right = sides(k, ds)
-
-            @pl.when(left)
-            def _():
-                relay(b - k, tb, right_copy, b < nb - 1)
-
-            @pl.when(right)
-            def _():
-                relay(b + k, tb, left_copy, b > 0)
-
-            @pl.when(left)
-            def _():
-                add_far(b - k, 0, tb)
-
-            @pl.when(right)
-            def _():
-                add_far(b + k, 1, tb)
-
-        if k == 1:
-            own_here = g_all.at[b, g_rows(s, c)]
-
-            def take_products(side):
-                y_z_copy(side, b).wait_recv()
-                add_product(b, y_far.at[side], own_here)
-
-            @pl.when(b == 1)
-            def _():
-                take_products(0)
-
-            @pl.when(b == nb - 2)
-            def _():
-                take_products(1)
+            add_blocks(k, ds)
+
+    own_here = g_all.at[b, g_rows(s, c)]
+
+    def take_products(side):
+        y_z_copy(side, b).wait_recv()
+        add_product(b, y_far.at[side], own_here)
+
+    @pl.when(b == 1)
+    def _():
+        take_products(0)
+
+    @pl.when(b == nb - 2)
+    def _():
+        take_products(1)
 
     mine[...] = jnp.concatenate([jnp.sum(part[j], axis=0, keepdims=True) for j in range(nb)], axis=0)
 
@@ -388,12 +420,9 @@
         tb = lax.rem(s + ds, ns)
         src = g_all.at[b, g_rows(tb, c)]
 
-        @pl.when(b < nb - 1)
+        @pl.when((b < nb - 1) & (b > 0))
         def _():
             right_copy(src, b, tb).wait_send()
-
-        @pl.when(b > 0)
-        def _():
             left_copy(src, b, tb).wait_send()
 
         side_copy(b, tb).wait_send()

time: 81.2 us -> 74.2 us (0.914)
  Pallas kernels: 79.2 us -> 72.2 us
    pallas_call x1, Pallas kernels: 79.2 us -> 72.2 us  [on_device(): pl.pallas_call(functools.partial(score_kernel, nb, ns, nc), out_shape=jax...]
where the time goes in v3:
time: 74.2 us; the launch traced here: 74 us
  Pallas kernels  72.2 us (97%)
  between operations  1.85 us (2%)
    pallas_call x1, Pallas kernels, on_device(): pl.pallas_call(functools.partial(score_kernel, nb, ns, nc), out_shape=jax...  72.2 us

profile of v3, /device:TPU:0, one launch (start us, length us, event | category | flops | bytes accessed | tf_op | source)
XLA Modules:
  0.0 74.0 jit_solution(6574942186854701787)
XLA Ops:
  0.7 72.2 %shard_map.55 = f32[1,1]{1,0:T(1,128)} custom-call(bf16[128,3456]{1,0:T(8,128)(2,1)} %a_ref.1, bf16[128,5120]{1,0:T(8,128)(2,1)} %g_ref.1, f32[1,864,2560]{2,1,0:T(8,128)} %q_ref.1, s32[1]{0:T(128)S(6)} %copy.7.length_ref, s32[4]{0:T(128)} %assign_ref.1), custom_call_target="tpu_custom_call" | custom-call | flops 4529848320 | bytes 8847360 | tf_op jit(solution)/shard_map/pallas_call | solution.py:476
